TPU v7x, 32 devices: a whole 2x2x4 slice. The times are simulated.
32 devices in a mesh: groups: 2 (over x), grid: 8 (over z, y), band: 2 (over core).
Axes of the slice: x: 2, y: 2, z: 4, core: 2. Of those that a mesh axis runs over, the one named last changes fastest.
Arguments:
- wavefunctions: bfloat16 [1024, 32768], P(('groups', 'grid', 'band')), parts along dimension 0, may hold values from -6 to 6
- tile_segment: int32 [3072], P('grid'), may hold values from 0 to 63
- tile_block: int32 [3072], P('grid'), may hold values from 0 to 31
- tile_count: int32 [8], P('grid'), may hold values from 48 to 384, as said below
- projectors: bfloat16 [3072, 64, 128], P('grid'), may hold values from -0.75 to 0.75
- coupling: float32 [32, 16, 8, 8], replicated, may hold values from -0.1875 to 0.1875
Outputs:
- applied_field: bfloat16 [1024, 32768], P(('groups', 'grid', 'band')), parts along dimension 0
There are 2 independent parts, one for each index of `groups`. A program takes and returns all parts, laid end to end along the dimension named above; an argument that names none is the same for every part. Nothing has to cross between parts.
Inputs may be any that keep to these rules, and one draw needn't show every extreme that they name: `tile_count`: some grid index has exactly 384 live slots; every other has 48 to 192.
All inputs are finite; a program needn't handle non-finite values.
Results may differ from a plain program's by a relative error of at most 0.0063.
Values may be sent and summed in bfloat16 or wider, within the bound.
No kernel may reach another device: no remote copies, remote signals or barrier semaphores. Data moves between devices by JAX's collectives and lax.ppermute only.
A program may use at most 128 MiB of HBM per device.

v0:
```python
import functools
import math

import jax
import jax.numpy as jnp
from jax import lax
from jax.experimental import pallas as pl
from jax.experimental.pallas import tpu as pltpu
from jax.sharding import PartitionSpec as P

TILE = 64
PAIR = 2 * TILE
GROUP = 4
UNROLL = 8
VMEM_SLACK = 10 * 1024 * 1024
PARTS = (19, 17, 12)
RANGES = ((0, 2), (2, 3))
OWN, OTHER = range(2)
BOUNDS = 3
STEPS = len(RANGES) + 1
LISTS = BOUNDS + 2 * STEPS


def bits(count):
    return max(1, (count - 1).bit_length())


def list_length(tiles, blocks):
    return tiles + len(RANGES) * ((GROUP - 1) * blocks + GROUP * UNROLL)


def group_lists(codes, keys, live, blocks, absent):
    n_lists, tiles = codes.shape
    n_keys = len(RANGES) * blocks
    order = jnp.arange(tiles, dtype=jnp.int32)
    key_range = jnp.arange(n_keys, dtype=jnp.int32)
    ranges = jnp.arange(STEPS, dtype=jnp.int32)
    mine = (keys[:, None, :] == key_range[None, :, None]) & live[:, None, :]
    groups = (jnp.sum(mine, axis=2, dtype=jnp.int32) + GROUP - 1) // GROUP
    in_range = key_range[:, None] // blocks == ranges[None, :]
    totals = jnp.sum(jnp.where(in_range, groups[:, :, None], 0), axis=1, dtype=jnp.int32)
    totals = (totals + UNROLL - 1) // UNROLL * UNROLL
    bounds = jnp.sum(
        jnp.where(ranges[:, None] < ranges[None, :], totals[:, :, None], 0), axis=1, dtype=jnp.int32
    )
    lower = (key_range[:, None] < key_range[None, :]) & (
        key_range[:, None] // blocks == key_range[None, :] // blocks
    )
    starts = jnp.sum(jnp.where(lower, groups[:, :, None], 0), axis=1, dtype=jnp.int32)
    starts += jnp.sum(jnp.where(in_range, bounds[:, None, :], 0), axis=2, dtype=jnp.int32)
    before = (
        (keys[:, :, None] == keys[:, None, :]) & live[:, :, None] & (order[:, None] < order[None, :])
    )
    entry = jnp.sum(before, axis=1, dtype=jnp.int32) + GROUP * jnp.sum(
        jnp.where(mine, starts[:, :, None], 0), axis=1, dtype=jnp.int32
    )
    entry = jnp.where(live, entry, -1)
    found = entry[:, :, None] == jnp.arange(list_length(tiles, blocks), dtype=jnp.int32)
    entries = absent + jnp.sum(
        jnp.where(found, codes[:, :, None] - absent, 0), axis=1, dtype=jnp.int32
    )
    return jnp.concatenate([bounds.reshape(-1), entries.reshape(-1)])


def group_loop(sizes, meta, values, proj, which, first, last, origin, product):
    tiles, segments, blocks = sizes
    begin, end = (meta[BOUNDS + STEPS * which + number] for number in (first, last))
    base = LISTS + which * list_length(tiles, blocks)

    def group(number):
        places = []
        for entry in range(GROUP):
            code = meta[base + GROUP * number + entry]
            index = jnp.maximum((code & ((1 << bits(tiles)) - 1)) - origin, 0)
            code = code >> bits(tiles)
            places.append((code & ((1 << bits(segments + 1)) - 1), values[index]))
            if entry == 0:
                block = code >> bits(segments + 1)
        lanes = pl.ds(pl.multiple_of(block * proj, proj), proj)
        return product(lanes, [at for at, tile in places], [tile for at, tile in places])

    def step(index, carry):
        sums = [group(begin + index * UNROLL + lane) for lane in range(UNROLL)]
        for additions in sums:
            for ref, rows, lanes, term in additions:
                ref[rows, lanes] += term
        return carry

    lax.fori_loop(0, (end - begin) // UNROLL, step, 0)


def join_pieces(meta, pieces, joined, first):
    end = 0
    for number, ref in enumerate(pieces):
        start, end = end, end + ref.shape[0]

        @pl.when(meta[2] > first + start - number % 4 * ref.shape[0])
        def copy(start=start, end=end, ref=ref):
            joined[start:end] = ref[...]


def rows_of(refs, lanes):
    return jnp.concatenate([ref[:, lanes] for ref in refs], axis=0)


def turn_waves(wave, turned, segments):
    for pair in range(segments // 2):
        values = wave[:, pair * PAIR : (pair + 1) * PAIR]
        turned[0, pair] = values
        turned[1, pair] = pltpu.roll(values.astype(jnp.float32), TILE, 1).astype(values.dtype)
    for way in range(2):
        turned[way, segments // 2] = jnp.zeros(turned.shape[2:], turned.dtype)


def project_kernel(sizes, n_pieces, spot, first, last, meta, wave, *refs):
    pieces, refs = refs[:n_pieces], refs[n_pieces:]
    turned, refs = refs[-1], refs[:-1]
    if not first:
        before, refs = refs[0], refs[1:]
    values = pieces[0]
    if n_pieces > 1:
        values, refs = refs[-1], refs[:-1]
        join_pieces(meta, pieces, values, spot[-1])
    total = refs[-1]
    total[...] = jnp.zeros_like(total) if first else before[...]
    every = slice(None)

    def product(lanes, segments, tiles):
        low = lax.broadcasted_iota(jnp.int32, turned.shape[2:], 1) < TILE
        waves = [
            jnp.where(
                low,
                turned[segments[at] & 1, segments[at] >> 1],
                turned[1 - (segments[at + 1] & 1), segments[at + 1] >> 1],
            )
            for at in range(0, GROUP, 2)
        ]
        term = jnp.dot(
            jnp.concatenate(waves, axis=1),
            jnp.concatenate(tiles, axis=0),
            preferred_element_type=jnp.float32,
        )
        return [(total, every, lanes, term)]

    @pl.when(meta[1 + spot[0]] > spot[-1])
    def loop():
        turn_waves(wave, turned, sizes[1])
        group_loop(sizes, meta, values, values.shape[2], *spot, product)

    if last:
        outs = refs[:-1]
        rows = outs[0].shape[0]
        for d, out in enumerate(outs):
            start = 0 if len(outs) == 1 else pl.multiple_of((meta[0] ^ d) * rows, rows)
            out[...] = total[pl.ds(start, rows), :].astype(out.dtype)


def spread_kernel(sizes, n_rows, n_pieces, which, meta, *refs):
    applied, refs = refs[:n_rows], refs[n_rows:]
    pieces, refs = refs[:n_pieces], refs[n_pieces:]
    values = pieces[0]
    if n_pieces > 1:
        values, refs = refs[-1], refs[:-1]
        join_pieces(meta, pieces, values, 0)
    outs, field = refs[:-1], refs[-1]
    field[...] = jnp.zeros_like(field)
    every = slice(None)

    def product(lanes, segments, tiles):
        terms = lax.dot_general(
            jnp.concatenate(tiles, axis=0),
            rows_of(applied, lanes),
            (((1,), (1,)), ((), ())),
            preferred_element_type=jnp.float32,
        )
        return [
            (
                field,
                pl.ds(pl.multiple_of(at * TILE, TILE), TILE),
                every,
                terms[number * TILE : (number + 1) * TILE],
            )
            for number, at in enumerate(segments)
        ]

    group_loop(sizes, meta, values, values.shape[2], which, 0, len(RANGES), 0, product)
    for pair in range(sizes[1] // 2):
        points = slice(pair * PAIR, (pair + 1) * PAIR)
        values, start = field[points, :].T, 0
        for out in outs:
            out[:, points] = values[start : start + out.shape[0]].astype(out.dtype)
            start += out.shape[0]


WHOLE = pl.BlockSpec(memory_space=pltpu.VMEM)


def cost(us):
    return pl.CostEstimate(flops=1 + us * 10**9, bytes_accessed=1, transcendentals=0)


def join_small(blocks):
    return blocks if blocks[0].shape[0] % 16 == 0 else [jnp.concatenate(blocks)]


def split_small(blocks, count):
    return blocks if len(blocks) == count else jnp.split(blocks[0], count)


def vmem(scratch):
    size = sum(math.prod(ref.shape) * jnp.dtype(ref.dtype).itemsize for ref in scratch)
    return pltpu.CompilerParams(vmem_limit_bytes=size + VMEM_SLACK)


def joined_shape(pieces):
    if len(pieces) == 1:
        return []
    count = sum(piece.shape[0] for piece in pieces)
    return [pltpu.VMEM((count,) + pieces[0].shape[1:], jnp.bfloat16)]


def project(sizes, meta, wave, pieces, count, width, spot, total=None, last=False, us=0):
    rows = wave.shape[0]
    operands = [wave, *pieces] + ([] if total is None else [total])
    scratch = joined_shape(pieces)
    scratch.append(pltpu.VMEM((2, sizes[1] // 2 + 1, rows, PAIR), jnp.bfloat16))
    if last:
        outs = count if rows // count % 16 == 0 else 1
        shapes = [jax.ShapeDtypeStruct((rows // outs, width), jnp.bfloat16)] * outs
        scratch = [pltpu.VMEM((rows, width), jnp.float32)] + scratch
    else:
        shapes = [jax.ShapeDtypeStruct((rows, width), jnp.float32)]
    result = pl.pallas_call(
        functools.partial(project_kernel, sizes, len(pieces), spot, total is None, last),
        grid_spec=pltpu.PrefetchScalarGridSpec(
            num_scalar_prefetch=1,
            grid=(1,),
            in_specs=[WHOLE] * len(operands),
            out_specs=[WHOLE] * len(shapes),
            scratch_shapes=scratch,
        ),
        out_shape=shapes,
        compiler_params=vmem(scratch),
        cost_estimate=cost(us),
    )(meta, *operands)
    return list(result) if last else result[0]


def spread(sizes, meta, applied, pieces, points, which):
    count = len(applied)
    applied = join_small(applied)
    rows = sum(block.shape[0] for block in applied)
    scratch = [pltpu.VMEM((points + TILE, rows), jnp.float32)] + joined_shape(pieces)
    result = pl.pallas_call(
        functools.partial(spread_kernel, sizes, len(applied), len(pieces), which),
        grid_spec=pltpu.PrefetchScalarGridSpec(
            num_scalar_prefetch=1,
            grid=(1,),
            in_specs=[WHOLE] * (len(applied) + len(pieces)),
            out_specs=[WHOLE] * len(applied),
            scratch_shapes=scratch,
        ),
        out_shape=[
            jax.ShapeDtypeStruct((block.shape[0], points), jnp.bfloat16) for block in applied
        ],
        compiler_params=vmem(scratch),
        cost_estimate=cost(0),
    )(meta, *applied, *pieces)
    return split_small(result, count)


def two_parts(values):
    high = values.astype(jnp.bfloat16)
    return high, (values - high.astype(jnp.float32)).astype(jnp.bfloat16)


def couple_kernel(high_ref, low_ref, *refs):
    parts, out_ref = refs[:-1], refs[-1]
    blocks, proj, unused = high_ref.shape
    for block in range(blocks):
        lanes = slice(block * proj, (block + 1) * proj)
        total = parts[0][:, lanes].astype(jnp.float32)
        for part in parts[1:]:
            total += part[:, lanes].astype(jnp.float32)
        high, low = two_parts(total)
        result = jnp.dot(high, high_ref[block], preferred_element_type=jnp.float32)
        result += jnp.dot(high, low_ref[block], preferred_element_type=jnp.float32)
        result += jnp.dot(low, high_ref[block], preferred_element_type=jnp.float32)
        out_ref[:, lanes] = result.astype(out_ref.dtype)


def couple(parts, high, low):
    return pl.pallas_call(
        couple_kernel,
        in_specs=[WHOLE] * (2 + len(parts)),
        out_specs=WHOLE,
        out_shape=jax.ShapeDtypeStruct(parts[0].shape, jnp.bfloat16),
        compiler_params=vmem([]),
        cost_estimate=cost(0),
    )(high, low, *parts)


def coupling_matrix(coupling):
    blocks, atoms, width, unused = coupling.shape
    proj = atoms * width
    wide = jnp.tile(coupling.reshape(blocks, proj, width), (1, 1, atoms))
    same = jnp.arange(proj)[:, None] // width == jnp.arange(proj)[None, :] // width
    return jnp.where(same[None], wide, 0.0)


def body(n_grid, wavefunctions, tile_segment, tile_block, tile_count, projectors, coupling):
    half = n_grid // 2
    bands, npts = wavefunctions.shape
    points = npts // n_grid
    tiles = projectors.shape[0]
    width = coupling.shape[0] * projectors.shape[2]
    index = lax.axis_index("grid")
    side, place = index // half, index % half
    group, core = lax.axis_index("groups"), lax.axis_index("band")
    partners = [(i, (i + half) % n_grid) for i in range(n_grid)]
    pools = [list(range(half)), list(range(half, n_grid))]
    swap = [(0, 1), (1, 0)]

    def exchange(blocks):
        return [blocks[0]] + [
            lax.ppermute(
                blocks[d], "grid", [(i, i // half * half + (i % half ^ d)) for i in range(n_grid)]
            )
            for d in range(1, half)
        ]

    def to_bricks(which):
        part = lax.dynamic_slice_in_dim(wavefunctions, which * half * points, half * points, 1)
        return lax.all_to_all(
            part, "grid", split_axis=1, concat_axis=0, tiled=True, axis_index_groups=pools
        )

    segments, blocks = points // TILE, coupling.shape[0]
    sizes = (tiles, segments, blocks)
    slots = jnp.arange(tiles, dtype=jnp.int32)
    starts = [tiles * sum(PARTS[:number]) // sum(PARTS) for number in range(len(PARTS) + 1)]
    held, range_of = slots, 0
    for start, end in zip(starts, starts[1:]):
        share = (end - start) // 4
        quarter, rest = (slots - start) // share, (slots - start) % share
        at = start + rest + share * ((quarter // 2 ^ group) + 2 * (quarter % 2 ^ core))
        held = jnp.where((slots >= start) & (slots < end), at, held)
    for first, end in RANGES[1:]:
        range_of += jnp.where(slots >= starts[first], 1, 0)

    own_wave = to_bricks(side)
    other_wave = to_bricks(1 - side)
    matrix = two_parts(coupling_matrix(coupling))

    arrived, pieces, across = [], [], None
    source = projectors
    for number, (start, end) in enumerate(zip(starts, starts[1:])):
        share = (end - start) // 4
        start += (2 * group + core) * share
        sent = lax.dynamic_slice_in_dim(source, start, share, 0)
        if number == 0:
            sent, source = lax.optimization_barrier((sent, source))
        if number > 0:
            sent = lax.optimization_barrier((sent, arrived[-1]))[0]
        arrived.append(lax.ppermute(sent, "grid", partners))

    numbers = jnp.stack([tile_segment, tile_block, jnp.broadcast_to(tile_count, (tiles,))])
    numbers = lax.optimization_barrier((numbers, arrived[0]))[0]
    others = lax.ppermute(numbers, "grid", partners)
    absent = segments << bits(tiles)
    segment, block = (jnp.stack([numbers[i], others[i]]) for i in (0, 1))
    codes = jnp.stack([slots, held])
    codes += (segment + (block << bits(segments + 1))) << bits(tiles)
    live = slots < jnp.stack([numbers[2], others[2]])
    keys = block + blocks * jnp.stack([jnp.zeros_like(slots), range_of])
    meta = jnp.concatenate(
        [
            jnp.stack([place, numbers[2, 0], others[2, 0]]),
            group_lists(codes, keys, live, blocks, absent),
        ]
    )

    own_wave = lax.optimization_barrier((own_wave, arrived[1]))[0]
    own_spot = (OWN, 0, len(RANGES), 0)
    total = project(sizes, meta, own_wave, [projectors], half, width, own_spot, us=2)
    for number, mine in enumerate(arrived):
        sent = mine
        if number == 1:
            sent, across, matrix = lax.optimization_barrier((sent, across, matrix))
        if number == 2:
            sent, across, other_wave, total = lax.optimization_barrier(
                (sent, across, other_wave, total)
            )
        across = lax.ppermute(sent, "groups", swap)
        pieces += [mine, across]
        pieces += [lax.ppermute(mine, "band", swap), lax.ppermute(across, "band", swap)]

    for number, (first, end) in enumerate(RANGES):
        last = end == len(PARTS)
        total = project(
            sizes,
            meta,
            other_wave,
            pieces[4 * first : 4 * end],
            half,
            width,
            (OTHER, number, number + 1, starts[first]),
            total,
            last=last,
            us=0 if last else 8,
        )
    if len(total) < half:
        total = [lax.dynamic_slice_in_dim(total[0], (place ^ d) * bands, bands, 0) for d in range(half)]

    applied = couple(exchange(total), *matrix)
    applied = exchange([applied] * half)

    result = jnp.zeros((bands, npts), jnp.bfloat16)
    for which, field in (
        (1 - side, spread(sizes, meta, applied, pieces, points, OTHER)),
        (side, spread(sizes, meta, applied, [projectors], points, OWN)),
    ):
        for d, block in enumerate(exchange(field)):
            start = (which * half + (place ^ d)) * points
            result = lax.dynamic_update_slice_in_dim(result, block, start, 1)
    return result


def solution(mesh):
    in_specs = (
        P(("groups", "grid", "band"), None),
        P("grid"),
        P("grid"),
        P("grid"),
        P("grid", None, None),
        P(),
    )
    out_specs = P(("groups", "grid", "band"), None)
    return jax.shard_map(
        functools.partial(body, mesh.shape["grid"]),
        mesh=mesh,
        in_specs=in_specs,
        out_specs=out_specs,
        check_vma=False,
    )
```

profile of v0, /device:TPU:0, one launch (start us, length us, event | category | flops | bytes accessed | tf_op | source)
XLA Modules:
  0.0 177.7 jit_solution(775968536518849425)
XLA Ops:
  0.0 2.6 %constant_dynamic-slice_fusion = (bf16[32,16384]{1,0:T(8,128)(2,1)S(1)}, bf16[32,16384]{1,0:T(8,128)(2,1)}) fusion(bf16[32,32768]{1,0:T(8,128)(2,1)} %param.6, s32[]{:T(128)S(6)} %select_n.386, s32[]{:T(128)S(6)} %select_n.385), kind=kLoop, calls=%fused_computation.50 | loop fusion | bytes 4194312 | tf_op jit(solution)/shard_map/dynamic_slice | solution.py:333
  3.7 5.4 %all-to-all-start.1 = ((bf16[32,4,4096]{2,0,1:T(8,128)(2,1)}), bf16[32,4,4096]{2,0,1:T(8,128)(2,1)S(1)}, u32[]{:S(2)}, u32[]{:S(2)}) async-start(bf16[32,4,4096]{2,0,1:T(8,128)(2,1)} %bitcast.19), calls=%async_computation.1 | async-start | bytes 2097152 | tf_op jit(solution)/shard_map/all_to_all | solution.py:334
  9.1 2.0 %constant_dynamic-slice_fusion.4 = bf16[38,64,128]{2,1,0:T(8,128)(2,1)} fusion(bf16[384,64,128]{2,1,0:T(8,128)(2,1)} %refs_4_.1, s32[]{:T(128)S(6)} %select_n.353), kind=kLoop, calls=%fused_computation.54 | loop fusion | bytes 1245188 | tf_op jit(solution)/shard_map/dynamic_slice | solution.py:360
  11.0 2.6 %collective-permute-start = (bf16[38,64,128]{2,1,0:T(8,128)(2,1)}, bf16[38,64,128]{2,1,0:T(8,128)(2,1)}, u32[]{:S(2)}, u32[]{:S(2)}) collective-permute-start(bf16[38,64,128]{2,1,0:T(8,128)(2,1)} %constant_dynamic-slice_fusion.4), channel_id=1, source_target_pairs={{0,8},{2,10},{4,12},{6,14},{8,0},{10,2},{12,4},{14,6},{1,9},{3,11}... | collective-permute-start | bytes 1867784 | tf_op jit(solution)/shard_map/ppermute | solution.py:365
  16.1 1.8 %copy.18 = f32[32,128,128]{2,1,0:T(8,128)} copy(f32[32,128,128]{1,2,0:T(8,128)S(1)} %broadcast_bitcast_fusion) | data formatting | bytes 4194304 | tf_op jit(solution)/shard_map/tile | solution.py:306
  18.0 1.9 %constant_dynamic-slice_fusion.2 = bf16[24,64,128]{2,1,0:T(8,128)(2,1)} fusion(bf16[384,64,128]{2,1,0:T(8,128)(2,1)} %refs_4_.1, s32[]{:T(128)S(6)} %select_n.383), kind=kLoop, calls=%fused_computation.52 | loop fusion | bytes 786436 | tf_op jit(solution)/shard_map/dynamic_slice | solution.py:360
  19.8 1.8 %select_convert_fusion.high_ref = bf16[32,128,128]{2,1,0:T(8,128)(2,1)S(1)} fusion(f32[32,128,128]{2,1,0:T(8,128)} %copy.18, pred[128,128]{1,0:T(8,128)(4,1)S(1)} %broadcast_compare_fusion), kind=kLoop, calls=%fused_computation.1 | loop fusion | flops 524288 | bytes 3162112 | tf_op jit(solution)/shard_map/convert_element_type | solution.py:273
  24.7 1.9 %constant_dynamic-slice_fusion.3 = bf16[34,64,128]{2,1,0:T(8,128)(2,1)} fusion(bf16[384,64,128]{2,1,0:T(8,128)(2,1)} %refs_4_.1, s32[]{:T(128)S(6)} %select_n.380), kind=kLoop, calls=%fused_computation.53 | loop fusion | bytes 1114116 | tf_op jit(solution)/shard_map/dynamic_slice | solution.py:360
  26.6 1.9 %subtract_convert_fusion.low_ref = bf16[32,128,128]{2,1,0:T(8,128)(2,1)S(1)} fusion(f32[32,128,128]{2,1,0:T(8,128)} %copy.18, pred[128,128]{1,0:T(8,128)(4,1)} %copy-done.16), kind=kLoop, calls=%fused_computation | loop fusion | flops 2621440 | bytes 3162112 | tf_op jit(solution)/shard_map/convert_element_type | solution.py:274
  28.5 12.6 %collective-permute-done.refs_0_.refs_4_ = bf16[38,64,128]{2,1,0:T(8,128)(2,1)} collective-permute-done((bf16[38,64,128]{2,1,0:T(8,128)(2,1)}, bf16[38,64,128]{2,1,0:T(8,128)(2,1)}, u32[]{:S(2)}, u32[]{:S(2)}) %collective-permute-start) | collective-permute-done | bytes 622624 | tf_op jit(solution)/shard_map/ppermute | solution.py:365
  41.7 2.9 %collective-permute-start.2 = (bf16[34,64,128]{2,1,0:T(8,128)(2,1)}, bf16[34,64,128]{2,1,0:T(8,128)(2,1)}, u32[]{:S(2)}, u32[]{:S(2)}) collective-permute-start(bf16[34,64,128]{2,1,0:T(8,128)(2,1)} %constant_dynamic-slice_fusion.3), channel_id=1, source_target_pairs={{0,8},{2,10},{4,12},{6,14},{8,0},{10,2},{12,4},{14,6},{1,9},{3,11}... | collective-permute-start | bytes 1671176 | tf_op jit(solution)/shard_map/ppermute | solution.py:365
  47.5 3.6 %all-to-all-start = ((bf16[32,4,4096]{2,0,1:T(8,128)(2,1)}), bf16[32,4,4096]{2,0,1:T(8,128)(2,1)S(1)}, u32[]{:S(2)}, u32[]{:S(2)}) async-start(bf16[32,4,4096]{2,0,1:T(8,128)(2,1)} %bitcast.26), calls=%async_computation | async-start | bytes 2097152 | tf_op jit(solution)/shard_map/all_to_all | solution.py:334
  51.9 16.4 %collective-permute-done.2.refs_4_.refs_8_ = bf16[34,64,128]{2,1,0:T(8,128)(2,1)} collective-permute-done((bf16[34,64,128]{2,1,0:T(8,128)(2,1)}, bf16[34,64,128]{2,1,0:T(8,128)(2,1)}, u32[]{:S(2)}, u32[]{:S(2)}) %collective-permute-start.2) | collective-permute-done | bytes 557088 | tf_op jit(solution)/shard_map/ppermute | solution.py:365
  74.1 2.0 %concatenate.26.meta = s32[1289]{0:T(1024)S(1)} concatenate(s32[1]{0:T(128)} %bitcast, s32[1]{0:T(128)} %bitcast.2, s32[1]{0:T(128)} %bitcast.3, s32[6]{0:T(128)} %reshape.790, s32[1280]{0:T(1024)S(1)} %add.465), dimensions={0} | concatenate | bytes 10312 | tf_op jit(solution)/shard_map/concatenate | solution.py:376
  76.6 4.4 %collective-permute-done.5.refs_5_.refs_9_ = bf16[34,64,128]{2,1,0:T(8,128)(2,1)} collective-permute-done((bf16[34,64,128]{2,1,0:T(8,128)(2,1)}, bf16[34,64,128]{2,1,0:T(8,128)(2,1)}, u32[]{:S(2)}, u32[]{:S(2)}) %collective-permute-start.5) | collective-permute-done | bytes 557088 | tf_op jit(solution)/shard_map/ppermute | solution.py:394
  81.1 2.8 %copy-done = bf16[384,64,128]{2,1,0:T(8,128)(2,1)S(1)} copy-done((bf16[384,64,128]{2,1,0:T(8,128)(2,1)S(1)}, bf16[384,64,128]{2,1,0:T(8,128)(2,1)}, u32[]{:S(2)}) %copy-start) | copy-done | bytes 6291480
  85.1 3.1 %shard_map.67.refs_8_ = f32[128,4096]{1,0:T(8,128)S(1)} custom-call(s32[1289]{0:T(1024)S(1)} %concatenate.26.meta, bf16[128,4096]{1,0:T(8,128)(2,1)S(1)} %bitcast.23, bf16[384,64,128]{2,1,0:T(8,128)(2,1)S(1)} %copy-done), custom_call_target="tpu_custom_call" | custom-call | flops 2000000000 | bytes 1 | tf_op jit(solution)/shard_map/pallas_call | solution.py:233
  91.3 9.8 %collective-permute-done.6.refs_1_.refs_13_ = bf16[24,64,128]{2,1,0:T(8,128)(2,1)S(1)} collective-permute-done((bf16[24,64,128]{2,1,0:T(8,128)(2,1)S(1)}, bf16[24,64,128]{2,1,0:T(8,128)(2,1)S(1)}, u32[]{:S(2)}, u32[]{:S(2)}) %collective-permute-start.6) | collective-permute-done | bytes 393248 | tf_op jit(solution)/shard_map/ppermute | solution.py:394
  102.8 6.5 %shard_map.68.refs_4_ = f32[128,4096]{1,0:T(8,128)S(1)} custom-call(s32[1289]{0:T(1024)S(1)} %concatenate.26.meta, bf16[128,4096]{1,0:T(8,128)(2,1)S(1)} %bitcast.21, bf16[38,64,128]{2,1,0:T(8,128)(2,1)} %collective-permute-done.refs_0_.refs_4_, bf16[38,64,128]{2,1,0:T(8,128)(2,1)} %collective-permute-done.3.refs_1_.refs_5_, ...), custom_call_target="tpu_custom_call" | custom-call | flops 8000000000 | bytes 1 | tf_op jit(solution)/shard_map/pallas_call | solution.py:233
  110.6 6.0 %collective-permute-start.14 = (bf16[32,4096]{1,0:T(8,128)(2,1)S(1)}, bf16[32,4096]{1,0:T(8,128)(2,1)S(1)}, u32[]{:S(2)}, u32[]{:S(2)}) collective-permute-start(bf16[32,4096]{1,0:T(8,128)(2,1)S(1)} %get-tuple-element.43), channel_id=1, source_target_pairs={{0,4},{2,6},{4,0},{6,2},{8,12},{10,14},{12,8},{14,10},{1,5},{3,7},... | collective-permute-start | bytes 786440 | tf_op jit(solution)/shard_map/ppermute | solution.py:326
  116.5 2.4 %collective-permute-done.13.refs_1_ = bf16[32,4096]{1,0:T(8,128)(2,1)S(1)} collective-permute-done((bf16[32,4096]{1,0:T(8,128)(2,1)S(1)}, bf16[32,4096]{1,0:T(8,128)(2,1)S(1)}, u32[]{:S(2)}, u32[]{:S(2)}) %collective-permute-start.13) | collective-permute-done | bytes 262176 | tf_op jit(solution)/shard_map/ppermute | solution.py:326
  118.9 4.7 %collective-permute-done.14.refs_2_ = bf16[32,4096]{1,0:T(8,128)(2,1)S(1)} collective-permute-done((bf16[32,4096]{1,0:T(8,128)(2,1)S(1)}, bf16[32,4096]{1,0:T(8,128)(2,1)S(1)}, u32[]{:S(2)}, u32[]{:S(2)}) %collective-permute-start.14) | collective-permute-done | bytes 262176 | tf_op jit(solution)/shard_map/ppermute | solution.py:326
  123.6 4.9 %collective-permute-done.15.refs_3_ = bf16[32,4096]{1,0:T(8,128)(2,1)S(1)} collective-permute-done((bf16[32,4096]{1,0:T(8,128)(2,1)S(1)}, bf16[32,4096]{1,0:T(8,128)(2,1)S(1)}, u32[]{:S(2)}, u32[]{:S(2)}) %collective-permute-start.15) | collective-permute-done | bytes 262176 | tf_op jit(solution)/shard_map/ppermute | solution.py:326
  132.9 4.8 %collective-permute-done.16.refs_1_ = bf16[32,4096]{1,0:T(8,128)(2,1)S(1)} collective-permute-done((bf16[32,4096]{1,0:T(8,128)(2,1)S(1)}, bf16[32,4096]{1,0:T(8,128)(2,1)S(1)}, u32[]{:S(2)}, u32[]{:S(2)}) %collective-permute-start.16) | collective-permute-done | bytes 262176 | tf_op jit(solution)/shard_map/ppermute | solution.py:326
  137.8 2.6 %collective-permute-done.17.refs_2_ = bf16[32,4096]{1,0:T(8,128)(2,1)S(1)} collective-permute-done((bf16[32,4096]{1,0:T(8,128)(2,1)S(1)}, bf16[32,4096]{1,0:T(8,128)(2,1)S(1)}, u32[]{:S(2)}, u32[]{:S(2)}) %collective-permute-start.17) | collective-permute-done | bytes 262176 | tf_op jit(solution)/shard_map/ppermute | solution.py:326
  140.4 3.9 %collective-permute-done.18.refs_3_ = bf16[32,4096]{1,0:T(8,128)(2,1)S(1)} collective-permute-done((bf16[32,4096]{1,0:T(8,128)(2,1)S(1)}, bf16[32,4096]{1,0:T(8,128)(2,1)S(1)}, u32[]{:S(2)}, u32[]{:S(2)}) %collective-permute-start.18) | collective-permute-done | bytes 262176 | tf_op jit(solution)/shard_map/ppermute | solution.py:326
  145.3 6.8 %shard_map.71 = (bf16[32,4096]{1,0:T(8,128)(2,1)S(1)}, bf16[32,4096]{1,0:T(8,128)(2,1)S(1)}, bf16[32,4096]{1,0:T(8,128)(2,1)S(1)}, bf16[32,4096]{1,0:T(8,128)(2,1)S(1)}) custom-call(s32[1289]{0:T(1024)S(1)} %concatenate.26.meta, bf16[32,4096]{1,0:T(8,128)(2,1)S(1)} %shard_map.70.refs_0_, bf16[32,4096]{1,0:T(8,128)(2,1)S(1)} %collective-permute-done.16.refs_1_, ...), custom_call_target="tpu_custom_call" | custom-call | flops 1 | bytes 1 | tf_op jit(solution)/shard_map/pallas_call | solution.py:254
  155.6 2.8 %copy-done.1 = bf16[384,64,128]{2,1,0:T(8,128)(2,1)S(1)} copy-done((bf16[384,64,128]{2,1,0:T(8,128)(2,1)S(1)}, bf16[384,64,128]{2,1,0:T(8,128)(2,1)}, u32[]{:S(2)}) %copy-start.1) | copy-done | bytes 6291480
  158.4 3.4 %shard_map.72 = (bf16[32,4096]{1,0:T(8,128)(2,1)S(1)}, bf16[32,4096]{1,0:T(8,128)(2,1)S(1)}, bf16[32,4096]{1,0:T(8,128)(2,1)S(1)}, bf16[32,4096]{1,0:T(8,128)(2,1)S(1)}) custom-call(s32[1289]{0:T(1024)S(1)} %concatenate.26.meta, bf16[32,4096]{1,0:T(8,128)(2,1)S(1)} %shard_map.70.refs_0_, bf16[32,4096]{1,0:T(8,128)(2,1)S(1)} %collective-permute-done.16.refs_1_, ...), custom_call_target="tpu_custom_call" | custom-call | flops 1 | bytes 1 | tf_op jit(solution)/shard_map/pallas_call | solution.py:254
  162.1 5.0 %collective-permute-start.23 = (bf16[32,4096]{1,0:T(8,128)(2,1)S(1)}, bf16[32,4096]{1,0:T(8,128)(2,1)S(1)}, u32[]{:S(2)}, u32[]{:S(2)}) collective-permute-start(bf16[32,4096]{1,0:T(8,128)(2,1)S(1)} %get-tuple-element.51), channel_id=1, source_target_pairs={{0,4},{2,6},{4,0},{6,2},{8,12},{10,14},{12,8},{14,10},{1,5},{3,7},... | collective-permute-start | bytes 786440 | tf_op jit(solution)/shard_map/ppermute | solution.py:326
  167.6 5.6 %collective-permute-done.22 = bf16[32,4096]{1,0:T(8,128)(2,1)S(1)} collective-permute-done((bf16[32,4096]{1,0:T(8,128)(2,1)S(1)}, bf16[32,4096]{1,0:T(8,128)(2,1)S(1)}, u32[]{:S(2)}, u32[]{:S(2)}) %collective-permute-start.22) | collective-permute-done | bytes 262176 | tf_op jit(solution)/shard_map/ppermute | solution.py:326
  173.5 3.5 %collective-permute-done.24 = bf16[32,4096]{1,0:T(8,128)(2,1)S(1)} collective-permute-done((bf16[32,4096]{1,0:T(8,128)(2,1)S(1)}, bf16[32,4096]{1,0:T(8,128)(2,1)S(1)}, u32[]{:S(2)}, u32[]{:S(2)}) %collective-permute-start.24) | collective-permute-done | bytes 262176 | tf_op jit(solution)/shard_map/ppermute | solution.py:326
  (136 shorter events, 34.2 us)
Async XLA Ops:
  3.7 42.8 %all-to-all-start.1 = ((bf16[32,4,4096]{2,0,1:T(8,128)(2,1)}), bf16[32,4,4096]{2,0,1:T(8,128)(2,1)S(1)}, u32[]{:S(2)}, u32[]{:S(2)}) async-start(bf16[32,4,4096]{2,0,1:T(8,128)(2,1)} %bitcast.19), calls=%async_computation.1 | async-start | bytes 2097152 | tf_op jit(solution)/shard_map/all_to_all | solution.py:334
  11.0 30.1 %collective-permute-start = (bf16[38,64,128]{2,1,0:T(8,128)(2,1)}, bf16[38,64,128]{2,1,0:T(8,128)(2,1)}, u32[]{:S(2)}, u32[]{:S(2)}) collective-permute-start(bf16[38,64,128]{2,1,0:T(8,128)(2,1)} %constant_dynamic-slice_fusion.4), channel_id=1, source_target_pairs={{0,8},{2,10},{4,12},{6,14},{8,0},{10,2},{12,4},{14,6},{1,9},{3,11}... | collective-permute-start | bytes 1867784 | tf_op jit(solution)/shard_map/ppermute | solution.py:365
  26.6 24.6 %copy-start.25 = (pred[3,3]{1,0:T(4,128)(4,1)S(1)}, pred[3,3]{1,0:T(4,128)(4,1)}, u32[]{:S(2)}) copy-start(pred[3,3]{1,0:T(4,128)(4,1)} %iota_compare_fusion.5) | copy-start | bytes 31
  26.6 25.1 %copy-start.14 = (pred[384,384]{1,0:T(8,128)(4,1)S(1)}, pred[384,384]{1,0:T(8,128)(4,1)}, u32[]{:S(2)}) copy-start(pred[384,384]{1,0:T(8,128)(4,1)} %iota_compare_fusion.1) | copy-start | bytes 442372
  41.1 5.0 %collective-permute-start.1 = (s32[3,384]{1,0:T(4,128)S(1)}, s32[3,384]{1,0:T(4,128)S(1)}, u32[]{:S(2)}, u32[]{:S(2)}) collective-permute-start(s32[3,384]{1,0:T(4,128)S(1)} %copy-done.17), channel_id=1, source_target_pairs={{0,8},{2,10},{4,12},{6,14},{8,0},{10,2},{12,4},{14,6},{1,9},{3,11}... | collective-permute-start | bytes 13832 | tf_op jit(solution)/shard_map/ppermute | solution.py:369
  41.7 26.7 %collective-permute-start.2 = (bf16[34,64,128]{2,1,0:T(8,128)(2,1)}, bf16[34,64,128]{2,1,0:T(8,128)(2,1)}, u32[]{:S(2)}, u32[]{:S(2)}) collective-permute-start(bf16[34,64,128]{2,1,0:T(8,128)(2,1)} %constant_dynamic-slice_fusion.3), channel_id=1, source_target_pairs={{0,8},{2,10},{4,12},{6,14},{8,0},{10,2},{12,4},{14,6},{1,9},{3,11}... | collective-permute-start | bytes 1671176 | tf_op jit(solution)/shard_map/ppermute | solution.py:365
  44.6 23.8 %collective-permute-start.3 = (bf16[38,64,128]{2,1,0:T(8,128)(2,1)}, bf16[38,64,128]{2,1,0:T(8,128)(2,1)}, u32[]{:S(2)}, u32[]{:S(2)}) collective-permute-start(bf16[38,64,128]{2,1,0:T(8,128)(2,1)} %collective-permute-done.refs_0_.refs_4_), channel_id=1, source_target_pairs={{0,16},{16,0},{1,17},{17,1},{2,18},{18,2},{3,19},{19,3},{4,20},{20... | collective-permute-start | bytes 1867784 | tf_op jit(solution)/shard_map/ppermute | solution.py:394
  46.1 44.9 %collective-permute-start.9 = (bf16[38,64,128]{2,1,0:T(8,128)(2,1)}, bf16[38,64,128]{2,1,0:T(8,128)(2,1)}, u32[]{:S(2)}, u32[]{:S(2)}) collective-permute-start(bf16[38,64,128]{2,1,0:T(8,128)(2,1)} %collective-permute-done.refs_0_.refs_4_), channel_id=1, source_target_pairs={{0,1},{1,0},{2,3},{3,2},{4,5},{5,4},{6,7},{7,6},{8,9},{9,8},{10,11... | collective-permute-start | bytes 1867784 | tf_op jit(solution)/shard_map/ppermute | solution.py:396
  46.1 23.8 %copy-start.21 = (s32[3,384]{1,0:T(4,128)}, s32[3,384]{1,0:T(4,128)S(1)}, u32[]{:S(2)}) copy-start(s32[3,384]{1,0:T(4,128)S(1)} %collective-permute-done.1) | copy-start | bytes 13828
  47.5 42.0 %all-to-all-start = ((bf16[32,4,4096]{2,0,1:T(8,128)(2,1)}), bf16[32,4,4096]{2,0,1:T(8,128)(2,1)S(1)}, u32[]{:S(2)}, u32[]{:S(2)}) async-start(bf16[32,4,4096]{2,0,1:T(8,128)(2,1)} %bitcast.26), calls=%async_computation | async-start | bytes 2097152 | tf_op jit(solution)/shard_map/all_to_all | solution.py:334
  68.4 12.7 %collective-permute-start.5 = (bf16[34,64,128]{2,1,0:T(8,128)(2,1)}, bf16[34,64,128]{2,1,0:T(8,128)(2,1)}, u32[]{:S(2)}, u32[]{:S(2)}) collective-permute-start(bf16[34,64,128]{2,1,0:T(8,128)(2,1)} %collective-permute-done.2.refs_4_.refs_8_), channel_id=1, source_target_pairs={{0,16},{16,0},{1,17},{17,1},{2,18},{18,2},{3,19},{19,3},{4,20},{20... | collective-permute-start | bytes 1671176 | tf_op jit(solution)/shard_map/ppermute | solution.py:394
  70.2 19.3 %collective-permute-start.4 = (bf16[24,64,128]{2,1,0:T(8,128)(2,1)}, bf16[24,64,128]{2,1,0:T(8,128)(2,1)S(1)}, u32[]{:S(2)}, u32[]{:S(2)}) collective-permute-start(bf16[24,64,128]{2,1,0:T(8,128)(2,1)} %constant_dynamic-slice_fusion.2), channel_id=1, source_target_pairs={{0,8},{2,10},{4,12},{6,14},{8,0},{10,2},{12,4},{14,6},{1,9},{3,11}... | collective-permute-start | bytes 1179656 | tf_op jit(solution)/shard_map/ppermute | solution.py:365
  70.3 30.8 %collective-permute-start.10 = (bf16[38,64,128]{2,1,0:T(8,128)(2,1)}, bf16[38,64,128]{2,1,0:T(8,128)(2,1)}, u32[]{:S(2)}, u32[]{:S(2)}) collective-permute-start(bf16[38,64,128]{2,1,0:T(8,128)(2,1)} %collective-permute-done.3.refs_1_.refs_5_), channel_id=1, source_target_pairs={{0,1},{1,0},{2,3},{3,2},{4,5},{5,4},{6,7},{7,6},{8,9},{9,8},{10,11... | collective-permute-start | bytes 1867784 | tf_op jit(solution)/shard_map/ppermute | solution.py:396
  76.1 24.9 %collective-permute-start.11 = (bf16[34,64,128]{2,1,0:T(8,128)(2,1)}, bf16[34,64,128]{2,1,0:T(8,128)(2,1)}, u32[]{:S(2)}, u32[]{:S(2)}) collective-permute-start(bf16[34,64,128]{2,1,0:T(8,128)(2,1)} %collective-permute-done.2.refs_4_.refs_8_), channel_id=1, source_target_pairs={{0,1},{1,0},{2,3},{3,2},{4,5},{5,4},{6,7},{7,6},{8,9},{9,8},{10,11... | collective-permute-start | bytes 1671176 | tf_op jit(solution)/shard_map/ppermute | solution.py:396
  81.1 20.0 %collective-permute-start.12 = (bf16[34,64,128]{2,1,0:T(8,128)(2,1)}, bf16[34,64,128]{2,1,0:T(8,128)(2,1)}, u32[]{:S(2)}, u32[]{:S(2)}) collective-permute-start(bf16[34,64,128]{2,1,0:T(8,128)(2,1)} %collective-permute-done.5.refs_5_.refs_9_), channel_id=1, source_target_pairs={{0,1},{1,0},{2,3},{3,2},{4,5},{5,4},{6,7},{7,6},{8,9},{9,8},{10,11... | collective-permute-start | bytes 1671176 | tf_op jit(solution)/shard_map/ppermute | solution.py:396
  89.5 11.5 %collective-permute-start.6 = (bf16[24,64,128]{2,1,0:T(8,128)(2,1)S(1)}, bf16[24,64,128]{2,1,0:T(8,128)(2,1)S(1)}, u32[]{:S(2)}, u32[]{:S(2)}) collective-permute-start(bf16[24,64,128]{2,1,0:T(8,128)(2,1)S(1)} %collective-permute-done.4.refs_0_.refs_12_), channel_id=1, source_target_pairs={{0,16},{16,0},{1,17},{17,1},{2,18},{18,2},{3,19},{19,3},{4,20},{20... | collective-permute-start | bytes 1179656 | tf_op jit(solution)/shard_map/ppermute | solution.py:394
  91.0 18.2 %collective-permute-start.7 = (bf16[24,64,128]{2,1,0:T(8,128)(2,1)S(1)}, bf16[24,64,128]{2,1,0:T(8,128)(2,1)S(1)}, u32[]{:S(2)}, u32[]{:S(2)}) collective-permute-start(bf16[24,64,128]{2,1,0:T(8,128)(2,1)S(1)} %collective-permute-done.4.refs_0_.refs_12_), channel_id=1, source_target_pairs={{0,1},{1,0},{2,3},{3,2},{4,5},{5,4},{6,7},{7,6},{8,9},{9,8},{10,11... | collective-permute-start | bytes 1179656 | tf_op jit(solution)/shard_map/ppermute | solution.py:396
  101.0 8.3 %collective-permute-start.8 = (bf16[24,64,128]{2,1,0:T(8,128)(2,1)S(1)}, bf16[24,64,128]{2,1,0:T(8,128)(2,1)S(1)}, u32[]{:S(2)}, u32[]{:S(2)}) collective-permute-start(bf16[24,64,128]{2,1,0:T(8,128)(2,1)S(1)} %collective-permute-done.6.refs_1_.refs_13_), channel_id=1, source_target_pairs={{0,1},{1,0},{2,3},{3,2},{4,5},{5,4},{6,7},{7,6},{8,9},{9,8},{10,11... | collective-permute-start | bytes 1179656 | tf_op jit(solution)/shard_map/ppermute | solution.py:396
  110.3 34.0 %copy-start.7 = (bf16[24,64,128]{2,1,0:T(8,128)(2,1)S(1)}, bf16[24,64,128]{2,1,0:T(8,128)(2,1)}, u32[]{:S(2)}) copy-start(bf16[24,64,128]{2,1,0:T(8,128)(2,1)} %copy-done.6) | copy-start | bytes 1179652
  110.3 34.0 %copy-start.9 = (bf16[24,64,128]{2,1,0:T(8,128)(2,1)S(1)}, bf16[24,64,128]{2,1,0:T(8,128)(2,1)}, u32[]{:S(2)}) copy-start(bf16[24,64,128]{2,1,0:T(8,128)(2,1)} %copy-done.8) | copy-start | bytes 1179652
  110.3 8.6 %collective-permute-start.13 = (bf16[32,4096]{1,0:T(8,128)(2,1)S(1)}, bf16[32,4096]{1,0:T(8,128)(2,1)S(1)}, u32[]{:S(2)}, u32[]{:S(2)}) collective-permute-start(bf16[32,4096]{1,0:T(8,128)(2,1)S(1)} %get-tuple-element.42), channel_id=1, source_target_pairs={{0,2},{2,0},{4,6},{6,4},{8,10},{10,8},{12,14},{14,12},{1,3},{3,1},... | collective-permute-start | bytes 786440 | tf_op jit(solution)/shard_map/ppermute | solution.py:326
  110.6 13.0 %collective-permute-start.14 = (bf16[32,4096]{1,0:T(8,128)(2,1)S(1)}, bf16[32,4096]{1,0:T(8,128)(2,1)S(1)}, u32[]{:S(2)}, u32[]{:S(2)}) collective-permute-start(bf16[32,4096]{1,0:T(8,128)(2,1)S(1)} %get-tuple-element.43), channel_id=1, source_target_pairs={{0,4},{2,6},{4,0},{6,2},{8,12},{10,14},{12,8},{14,10},{1,5},{3,7},... | collective-permute-start | bytes 786440 | tf_op jit(solution)/shard_map/ppermute | solution.py:326
  116.5 12.0 %collective-permute-start.15 = (bf16[32,4096]{1,0:T(8,128)(2,1)S(1)}, bf16[32,4096]{1,0:T(8,128)(2,1)S(1)}, u32[]{:S(2)}, u32[]{:S(2)}) collective-permute-start(bf16[32,4096]{1,0:T(8,128)(2,1)S(1)} %get-tuple-element.44), channel_id=1, source_target_pairs={{0,6},{2,4},{4,2},{6,0},{8,14},{10,12},{12,10},{14,8},{1,7},{3,5},... | collective-permute-start | bytes 786440 | tf_op jit(solution)/shard_map/ppermute | solution.py:326
  129.4 8.3 %collective-permute-start.16 = (bf16[32,4096]{1,0:T(8,128)(2,1)S(1)}, bf16[32,4096]{1,0:T(8,128)(2,1)S(1)}, u32[]{:S(2)}, u32[]{:S(2)}) collective-permute-start(bf16[32,4096]{1,0:T(8,128)(2,1)S(1)} %shard_map.70.refs_0_), channel_id=1, source_target_pairs={{0,2},{2,0},{4,6},{6,4},{8,10},{10,8},{12,14},{14,12},{1,3},{3,1},... | collective-permute-start | bytes 786440 | tf_op jit(solution)/shard_map/ppermute | solution.py:326
  131.1 9.2 %collective-permute-start.17 = (bf16[32,4096]{1,0:T(8,128)(2,1)S(1)}, bf16[32,4096]{1,0:T(8,128)(2,1)S(1)}, u32[]{:S(2)}, u32[]{:S(2)}) collective-permute-start(bf16[32,4096]{1,0:T(8,128)(2,1)S(1)} %shard_map.70.refs_0_), channel_id=1, source_target_pairs={{0,4},{2,6},{4,0},{6,2},{8,12},{10,14},{12,8},{14,10},{1,5},{3,7},... | collective-permute-start | bytes 786440 | tf_op jit(solution)/shard_map/ppermute | solution.py:326
  132.9 11.4 %collective-permute-start.18 = (bf16[32,4096]{1,0:T(8,128)(2,1)S(1)}, bf16[32,4096]{1,0:T(8,128)(2,1)S(1)}, u32[]{:S(2)}, u32[]{:S(2)}) collective-permute-start(bf16[32,4096]{1,0:T(8,128)(2,1)S(1)} %shard_map.70.refs_0_), channel_id=1, source_target_pairs={{0,6},{2,4},{4,2},{6,0},{8,14},{10,12},{12,10},{14,8},{1,7},{3,5},... | collective-permute-start | bytes 786440 | tf_op jit(solution)/shard_map/ppermute | solution.py:326
  152.1 15.3 %collective-permute-start.19 = (bf16[32,4096]{1,0:T(8,128)(2,1)S(1)}, bf16[32,4096]{1,0:T(8,128)(2,1)S(1)}, u32[]{:S(2)}, u32[]{:S(2)}) collective-permute-start(bf16[32,4096]{1,0:T(8,128)(2,1)S(1)} %get-tuple-element.46), channel_id=1, source_target_pairs={{0,2},{2,0},{4,6},{6,4},{8,10},{10,8},{12,14},{14,12},{1,3},{3,1},... | collective-permute-start | bytes 786440 | tf_op jit(solution)/shard_map/ppermute | solution.py:326
  153.1 14.3 %collective-permute-start.20 = (bf16[32,4096]{1,0:T(8,128)(2,1)S(1)}, bf16[32,4096]{1,0:T(8,128)(2,1)S(1)}, u32[]{:S(2)}, u32[]{:S(2)}) collective-permute-start(bf16[32,4096]{1,0:T(8,128)(2,1)S(1)} %get-tuple-element.47), channel_id=1, source_target_pairs={{0,4},{2,6},{4,0},{6,2},{8,12},{10,14},{12,8},{14,10},{1,5},{3,7},... | collective-permute-start | bytes 786440 | tf_op jit(solution)/shard_map/ppermute | solution.py:326
  154.5 13.0 %collective-permute-start.21 = (bf16[32,4096]{1,0:T(8,128)(2,1)S(1)}, bf16[32,4096]{1,0:T(8,128)(2,1)S(1)}, u32[]{:S(2)}, u32[]{:S(2)}) collective-permute-start(bf16[32,4096]{1,0:T(8,128)(2,1)S(1)} %get-tuple-element.48), channel_id=1, source_target_pairs={{0,6},{2,4},{4,2},{6,0},{8,14},{10,12},{12,10},{14,8},{1,7},{3,5},... | collective-permute-start | bytes 786440 | tf_op jit(solution)/shard_map/ppermute | solution.py:326
  161.8 11.4 %collective-permute-start.22 = (bf16[32,4096]{1,0:T(8,128)(2,1)S(1)}, bf16[32,4096]{1,0:T(8,128)(2,1)S(1)}, u32[]{:S(2)}, u32[]{:S(2)}) collective-permute-start(bf16[32,4096]{1,0:T(8,128)(2,1)S(1)} %get-tuple-element.50), channel_id=1, source_target_pairs={{0,2},{2,0},{4,6},{6,4},{8,10},{10,8},{12,14},{14,12},{1,3},{3,1},... | collective-permute-start | bytes 786440 | tf_op jit(solution)/shard_map/ppermute | solution.py:326
  162.1 11.4 %collective-permute-start.23 = (bf16[32,4096]{1,0:T(8,128)(2,1)S(1)}, bf16[32,4096]{1,0:T(8,128)(2,1)S(1)}, u32[]{:S(2)}, u32[]{:S(2)}) collective-permute-start(bf16[32,4096]{1,0:T(8,128)(2,1)S(1)} %get-tuple-element.51), channel_id=1, source_target_pairs={{0,4},{2,6},{4,0},{6,2},{8,12},{10,14},{12,8},{14,10},{1,5},{3,7},... | collective-permute-start | bytes 786440 | tf_op jit(solution)/shard_map/ppermute | solution.py:326
  167.4 9.7 %collective-permute-start.24 = (bf16[32,4096]{1,0:T(8,128)(2,1)S(1)}, bf16[32,4096]{1,0:T(8,128)(2,1)S(1)}, u32[]{:S(2)}, u32[]{:S(2)}) collective-permute-start(bf16[32,4096]{1,0:T(8,128)(2,1)S(1)} %get-tuple-element.52), channel_id=1, source_target_pairs={{0,6},{2,4},{4,2},{6,0},{8,14},{10,12},{12,10},{14,8},{1,7},{3,5},... | collective-permute-start | bytes 786440 | tf_op jit(solution)/shard_map/ppermute | solution.py:326
  (21 other events, 172.3 us)
where the time goes:
time: 180 us; the launch traced here: 178 us
  waiting for transfers between devices  75.9 us (42%)
  starting transfers between devices  38.7 us (22%)
  local copies, waits for them, and re-layouts  31.4 us (17%)
  Pallas kernels  21.6 us (12%)
  other arithmetic  8.96 us (5%)
    ppermute x12, waiting for transfers between devices, exchange(): lax.ppermute(blocks[d], 'grid', [(i, i // half * half + (i % half ^ d)) f...  32.7 us
    ppermute x3, waiting for transfers between devices, body(): arrived.append(lax.ppermute(sent, 'grid', partners))  29 us
    ppermute x12, starting transfers between devices, exchange(): lax.ppermute(blocks[d], 'grid', [(i, i // half * half + (i % half ^ d)) f...  18.8 us
    ppermute x3, waiting for transfers between devices, body(): across = lax.ppermute(sent, 'groups', swap)  14.2 us
    unnamed x52, local copies, waits for them, and re-layouts  11.9 us
    pallas_call x3, Pallas kernels, project(): pl.pallas_call(functools.partial(project_kernel, sizes, len(pieces), spot...  10.5 us
    pallas_call x2, Pallas kernels, spread(): pl.pallas_call(functools.partial(spread_kernel, sizes, len(applied), len(...  10.2 us
    all_to_all x2, starting transfers between devices, to_bricks(): lax.all_to_all(part, 'grid', split_axis=1, concat_axis=0, tiled=True, axi...  9.02 us
  transfers between devices with their start and end apart: 27, of which 13 were waited for; matrix products, arithmetic and copies ran while one was open for 14% of the time, Pallas kernels for 7%

commit v1 on v0

--- a/solution.py
+++ b/solution.py
@@ -13,7 +13,7 @@
 GROUP = 4
 UNROLL = 8
 VMEM_SLACK = 10 * 1024 * 1024
-PARTS = (19, 17, 12)
+PARTS = (15, 17, 16)
 RANGES = ((0, 2), (2, 3))
 OWN, OTHER = range(2)
 BOUNDS = 3
@@ -329,8 +329,9 @@
             for d in range(1, half)
         ]
 
-    def to_bricks(which):
+    def to_bricks(which, after):
         part = lax.dynamic_slice_in_dim(wavefunctions, which * half * points, half * points, 1)
+        part = lax.optimization_barrier((part, after))[0]
         return lax.all_to_all(
             part, "grid", split_axis=1, concat_axis=0, tiled=True, axis_index_groups=pools
         )
@@ -348,8 +349,6 @@
     for first, end in RANGES[1:]:
         range_of += jnp.where(slots >= starts[first], 1, 0)
 
-    own_wave = to_bricks(side)
-    other_wave = to_bricks(1 - side)
     matrix = two_parts(coupling_matrix(coupling))
 
     arrived, pieces, across = [], [], None
@@ -361,7 +360,7 @@
         if number == 0:
             sent, source = lax.optimization_barrier((sent, source))
         if number > 0:
-            sent = lax.optimization_barrier((sent, arrived[-1]))[0]
+            sent = lax.optimization_barrier((sent, arrived[0]))[0]
         arrived.append(lax.ppermute(sent, "grid", partners))
 
     numbers = jnp.stack([tile_segment, tile_block, jnp.broadcast_to(tile_count, (tiles,))])
@@ -380,7 +379,8 @@
         ]
     )
 
-    own_wave = lax.optimization_barrier((own_wave, arrived[1]))[0]
+    own_wave = to_bricks(side, arrived[0])
+    other_wave = to_bricks(1 - side, own_wave)
     own_spot = (OWN, 0, len(RANGES), 0)
     total = project(sizes, meta, own_wave, [projectors], half, width, own_spot, us=2)
     for number, mine in enumerate(arrived):

time: 180 us -> 196 us (1.089)
  waiting for transfers between devices: 75.9 us -> 92.5 us
  other arithmetic: 8.96 us -> 3.79 us
  local copies, waits for them, and re-layouts: 31.4 us -> 35.3 us
    all_to_all x2, waiting for transfers between devices: 0.01 us -> 6.09 us  [to_bricks(): lax.all_to_all(part, 'grid', split_axis=1, concat_axis=0, tiled=True, axi...]
    ppermute x3, waiting for transfers between devices: 14.2 us -> 18.9 us  [body(): across = lax.ppermute(sent, 'groups', swap)]
    ppermute x1, starting transfers between devices: 0.01 us -> 2.84 us  [body(): others = lax.ppermute(numbers, 'grid', partners)]
    another operation x3, local copies, waits for them, and re-layouts: 2.17 us -> 4.6 us  [coupling_matrix(): wide = jnp.tile(coupling.reshape(blocks, proj, width), (1, 1, atoms))]
    all_to_all x2, starting transfers between devices: 9.02 us -> 7.03 us  [to_bricks(): lax.all_to_all(part, 'grid', split_axis=1, concat_axis=0, tiled=True, axi...]
    unnamed x52 -> x36, local copies, waits for them, and re-layouts: 11.9 us -> 13.2 us
  transfers between devices with their start and end apart: 27 -> 27, of which waited for: 13 -> 17; matrix products, arithmetic and copies ran while one was open for 14% -> 12% of each run, Pallas kernels for 7% -> 6%
where the time goes in v1:
time: 196 us; the launch traced here: 193 us
  waiting for transfers between devices  92.5 us (47%)
  starting transfers between devices  39.6 us (20%)
  local copies, waits for them, and re-layouts  35.3 us (18%)
  Pallas kernels  20.4 us (10%)
  other arithmetic  3.79 us (2%)
    ppermute x12, waiting for transfers between devices, exchange(): lax.ppermute(blocks[d], 'grid', [(i, i // half * half + (i % half ^ d)) f...  34.1 us
    ppermute x3, waiting for transfers between devices, body(): arrived.append(lax.ppermute(sent, 'grid', partners))  30.8 us
    ppermute x3, waiting for transfers between devices, body(): across = lax.ppermute(sent, 'groups', swap)  18.9 us
    ppermute x12, starting transfers between devices, exchange(): lax.ppermute(blocks[d], 'grid', [(i, i // half * half + (i % half ^ d)) f...  17.5 us
    unnamed x36, local copies, waits for them, and re-layouts  13.2 us
    pallas_call x3, Pallas kernels, project(): pl.pallas_call(functools.partial(project_kernel, sizes, len(pieces), spot...  10.4 us
    pallas_call x2, Pallas kernels, spread(): pl.pallas_call(functools.partial(spread_kernel, sizes, len(applied), len(...  9.09 us
    all_to_all x2, starting transfers between devices, to_bricks(): lax.all_to_all(part, 'grid', split_axis=1, concat_axis=0, tiled=True, axi...  7.03 us
  transfers between devices with their start and end apart: 27, of which 17 were waited for; matrix products, arithmetic and copies ran while one was open for 12% of the time, Pallas kernels for 6%

profile of v1, /device:TPU:0, one launch (start us, length us, event | category | flops | bytes accessed | tf_op | source)
XLA Modules:
  0.0 192.7 jit_solution(9315641680565525138)
XLA Ops:
  1.9 4.0 %collective-permute-start = (bf16[30,64,128]{2,1,0:T(8,128)(2,1)}, bf16[30,64,128]{2,1,0:T(8,128)(2,1)}, u32[]{:S(2)}, u32[]{:S(2)}) collective-permute-start(bf16[30,64,128]{2,1,0:T(8,128)(2,1)} %constant_dynamic-slice_fusion.4), channel_id=1, source_target_pairs={{0,8},{2,10},{4,12},{6,14},{8,0},{10,2},{12,4},{14,6},{1,9},{3,11}... | collective-permute-start | bytes 1474568 | tf_op jit(solution)/shard_map/ppermute | solution.py:364
  12.9 2.3 %constant_dynamic-slice_fusion.2 = bf16[32,64,128]{2,1,0:T(8,128)(2,1)} fusion(bf16[384,64,128]{2,1,0:T(8,128)(2,1)} %refs_4_.1, s32[]{:T(128)S(6)} %select_n.383), kind=kLoop, calls=%fused_computation.55 | loop fusion | bytes 1048580 | tf_op jit(solution)/shard_map/dynamic_slice | solution.py:359
  15.2 2.7 %constant_dynamic-slice_fusion = (bf16[32,16384]{1,0:T(8,128)(2,1)S(1)}, bf16[32,16384]{1,0:T(8,128)(2,1)}) fusion(bf16[32,32768]{1,0:T(8,128)(2,1)} %param.6, s32[]{:T(128)S(6)} %select_n.386, s32[]{:T(128)S(6)} %select_n.385), kind=kLoop, calls=%fused_computation.53 | loop fusion | bytes 4194312 | tf_op jit(solution)/shard_map/dynamic_slice | solution.py:333
  18.2 9.8 %collective-permute-done.refs_0_.refs_4_ = bf16[30,64,128]{2,1,0:T(8,128)(2,1)} collective-permute-done((bf16[30,64,128]{2,1,0:T(8,128)(2,1)}, bf16[30,64,128]{2,1,0:T(8,128)(2,1)}, u32[]{:S(2)}, u32[]{:S(2)}) %collective-permute-start) | collective-permute-done | bytes 491552 | tf_op jit(solution)/shard_map/ppermute | solution.py:364
  29.0 3.5 %all-to-all-start = ((bf16[32,4,4096]{2,0,1:T(8,128)(2,1)}), bf16[32,4,4096]{2,0,1:T(8,128)(2,1)S(1)}, u32[]{:S(2)}, u32[]{:S(2)}) async-start(bf16[32,4,4096]{2,0,1:T(8,128)(2,1)} %bitcast.20), calls=%async_computation | async-start | bytes 2097152 | tf_op jit(solution)/shard_map/all_to_all | solution.py:335
  36.3 2.8 %collective-permute-start.1 = (s32[3,384]{1,0:T(4,128)S(1)}, s32[3,384]{1,0:T(4,128)S(1)}, u32[]{:S(2)}, u32[]{:S(2)}) collective-permute-start(s32[3,384]{1,0:T(4,128)S(1)} %add_add_fusion), channel_id=1, source_target_pairs={{0,8},{2,10},{4,12},{6,14},{8,0},{10,2},{12,4},{14,6},{1,9},{3,11}... | collective-permute-start | bytes 13832 | tf_op jit(solution)/shard_map/ppermute | solution.py:368
  39.9 2.8 %collective-permute-start.4 = (bf16[32,64,128]{2,1,0:T(8,128)(2,1)}, bf16[32,64,128]{2,1,0:T(8,128)(2,1)}, u32[]{:S(2)}, u32[]{:S(2)}) collective-permute-start(bf16[32,64,128]{2,1,0:T(8,128)(2,1)} %constant_dynamic-slice_fusion.2), channel_id=1, source_target_pairs={{0,8},{2,10},{4,12},{6,14},{8,0},{10,2},{12,4},{14,6},{1,9},{3,11}... | collective-permute-start | bytes 1572872 | tf_op jit(solution)/shard_map/ppermute | solution.py:364
  45.6 6.1 %all-to-all-done = bf16[32,4,4096]{2,0,1:T(8,128)(2,1)S(1)} async-done(((bf16[32,4,4096]{2,0,1:T(8,128)(2,1)}), bf16[32,4,4096]{2,0,1:T(8,128)(2,1)S(1)}, u32[]{:S(2)}, u32[]{:S(2)}) %all-to-all-start) | async-done | bytes 1048608 | tf_op jit(solution)/shard_map/all_to_all | solution.py:335
  51.7 2.7 %copy.23 = bf16[4,4,8,4096]{3,2,0,1:T(8,128)(2,1)} copy(bf16[4,4,8,4096]{3,2,1,0:T(8,128)(2,1)} %bitcast.24) | data formatting | bytes 2097152 | tf_op jit(solution)/shard_map/all_to_all | solution.py:335
  54.4 3.5 %all-to-all-start.1 = ((bf16[32,4,4096]{2,0,1:T(8,128)(2,1)}), bf16[32,4,4096]{2,0,1:T(8,128)(2,1)S(1)}, u32[]{:S(2)}, u32[]{:S(2)}) async-start(bf16[32,4,4096]{2,0,1:T(8,128)(2,1)} %bitcast.26), calls=%async_computation.1 | async-start | bytes 2097152 | tf_op jit(solution)/shard_map/all_to_all | solution.py:335
  58.8 21.1 %collective-permute-done.2.refs_4_.refs_8_ = bf16[34,64,128]{2,1,0:T(8,128)(2,1)} collective-permute-done((bf16[34,64,128]{2,1,0:T(8,128)(2,1)}, bf16[34,64,128]{2,1,0:T(8,128)(2,1)}, u32[]{:S(2)}, u32[]{:S(2)}) %collective-permute-start.2) | collective-permute-done | bytes 557088 | tf_op jit(solution)/shard_map/ppermute | solution.py:364
  83.6 8.1 %collective-permute-done.5.refs_5_.refs_9_ = bf16[34,64,128]{2,1,0:T(8,128)(2,1)} collective-permute-done((bf16[34,64,128]{2,1,0:T(8,128)(2,1)}, bf16[34,64,128]{2,1,0:T(8,128)(2,1)}, u32[]{:S(2)}, u32[]{:S(2)}) %collective-permute-start.5) | collective-permute-done | bytes 557088 | tf_op jit(solution)/shard_map/ppermute | solution.py:394
  91.8 2.8 %copy-done = bf16[384,64,128]{2,1,0:T(8,128)(2,1)S(1)} copy-done((bf16[384,64,128]{2,1,0:T(8,128)(2,1)S(1)}, bf16[384,64,128]{2,1,0:T(8,128)(2,1)}, u32[]{:S(2)}) %copy-start) | copy-done | bytes 6291480
  95.8 2.8 %shard_map.67.refs_8_ = f32[128,4096]{1,0:T(8,128)S(1)} custom-call(s32[1289]{0:T(1024)S(1)} %concatenate.26.meta, bf16[128,4096]{1,0:T(8,128)(2,1)S(1)} %bitcast.23, bf16[384,64,128]{2,1,0:T(8,128)(2,1)S(1)} %copy-done), custom_call_target="tpu_custom_call" | custom-call | flops 2000000000 | bytes 1 | tf_op jit(solution)/shard_map/pallas_call | solution.py:233
  103.7 10.7 %collective-permute-done.6.refs_1_.refs_13_ = bf16[32,64,128]{2,1,0:T(8,128)(2,1)S(1)} collective-permute-done((bf16[32,64,128]{2,1,0:T(8,128)(2,1)}, bf16[32,64,128]{2,1,0:T(8,128)(2,1)S(1)}, u32[]{:S(2)}, u32[]{:S(2)}) %collective-permute-start.6) | collective-permute-done | bytes 524320 | tf_op jit(solution)/shard_map/ppermute | solution.py:394
  114.5 1.9 copy-done.11
  116.4 5.7 %shard_map.68.refs_4_ = f32[128,4096]{1,0:T(8,128)S(1)} custom-call(s32[1289]{0:T(1024)S(1)} %concatenate.26.meta, bf16[128,4096]{1,0:T(8,128)(2,1)S(1)} %bitcast.21, bf16[30,64,128]{2,1,0:T(8,128)(2,1)} %collective-permute-done.refs_0_.refs_4_, bf16[30,64,128]{2,1,0:T(8,128)(2,1)} %collective-permute-done.3.refs_1_.refs_5_, ...), custom_call_target="tpu_custom_call" | custom-call | flops 8000000000 | bytes 1 | tf_op jit(solution)/shard_map/pallas_call | solution.py:233
  124.8 3.1 %collective-permute-start.14 = (bf16[32,4096]{1,0:T(8,128)(2,1)S(1)}, bf16[32,4096]{1,0:T(8,128)(2,1)S(1)}, u32[]{:S(2)}, u32[]{:S(2)}) collective-permute-start(bf16[32,4096]{1,0:T(8,128)(2,1)S(1)} %get-tuple-element.45), channel_id=1, source_target_pairs={{0,4},{2,6},{4,0},{6,2},{8,12},{10,14},{12,8},{14,10},{1,5},{3,7},... | collective-permute-start | bytes 786440 | tf_op jit(solution)/shard_map/ppermute | solution.py:326
  127.9 4.8 %collective-permute-done.13.refs_1_ = bf16[32,4096]{1,0:T(8,128)(2,1)S(1)} collective-permute-done((bf16[32,4096]{1,0:T(8,128)(2,1)S(1)}, bf16[32,4096]{1,0:T(8,128)(2,1)S(1)}, u32[]{:S(2)}, u32[]{:S(2)}) %collective-permute-start.13) | collective-permute-done | bytes 262176 | tf_op jit(solution)/shard_map/ppermute | solution.py:326
  132.7 2.3 %collective-permute-done.14.refs_2_ = bf16[32,4096]{1,0:T(8,128)(2,1)S(1)} collective-permute-done((bf16[32,4096]{1,0:T(8,128)(2,1)S(1)}, bf16[32,4096]{1,0:T(8,128)(2,1)S(1)}, u32[]{:S(2)}, u32[]{:S(2)}) %collective-permute-start.14) | collective-permute-done | bytes 262176 | tf_op jit(solution)/shard_map/ppermute | solution.py:326
  135.0 4.8 %collective-permute-done.15.refs_3_ = bf16[32,4096]{1,0:T(8,128)(2,1)S(1)} collective-permute-done((bf16[32,4096]{1,0:T(8,128)(2,1)S(1)}, bf16[32,4096]{1,0:T(8,128)(2,1)S(1)}, u32[]{:S(2)}, u32[]{:S(2)}) %collective-permute-start.15) | collective-permute-done | bytes 262176 | tf_op jit(solution)/shard_map/ppermute | solution.py:326
  144.3 4.8 %collective-permute-done.16.refs_1_ = bf16[32,4096]{1,0:T(8,128)(2,1)S(1)} collective-permute-done((bf16[32,4096]{1,0:T(8,128)(2,1)S(1)}, bf16[32,4096]{1,0:T(8,128)(2,1)S(1)}, u32[]{:S(2)}, u32[]{:S(2)}) %collective-permute-start.16) | collective-permute-done | bytes 262176 | tf_op jit(solution)/shard_map/ppermute | solution.py:326
  149.1 2.6 %collective-permute-done.17.refs_2_ = bf16[32,4096]{1,0:T(8,128)(2,1)S(1)} collective-permute-done((bf16[32,4096]{1,0:T(8,128)(2,1)S(1)}, bf16[32,4096]{1,0:T(8,128)(2,1)S(1)}, u32[]{:S(2)}, u32[]{:S(2)}) %collective-permute-start.17) | collective-permute-done | bytes 262176 | tf_op jit(solution)/shard_map/ppermute | solution.py:326
  151.7 3.7 %collective-permute-done.18.refs_3_ = bf16[32,4096]{1,0:T(8,128)(2,1)S(1)} collective-permute-done((bf16[32,4096]{1,0:T(8,128)(2,1)S(1)}, bf16[32,4096]{1,0:T(8,128)(2,1)S(1)}, u32[]{:S(2)}, u32[]{:S(2)}) %collective-permute-start.18) | collective-permute-done | bytes 262176 | tf_op jit(solution)/shard_map/ppermute | solution.py:326
  158.5 6.1 %shard_map.71 = (bf16[32,4096]{1,0:T(8,128)(2,1)S(1)}, bf16[32,4096]{1,0:T(8,128)(2,1)S(1)}, bf16[32,4096]{1,0:T(8,128)(2,1)S(1)}, bf16[32,4096]{1,0:T(8,128)(2,1)S(1)}) custom-call(s32[1289]{0:T(1024)S(1)} %concatenate.26.meta, bf16[32,4096]{1,0:T(8,128)(2,1)S(1)} %shard_map.70.refs_0_, bf16[32,4096]{1,0:T(8,128)(2,1)S(1)} %collective-permute-done.16.refs_1_, ...), custom_call_target="tpu_custom_call" | custom-call | flops 1 | bytes 1 | tf_op jit(solution)/shard_map/pallas_call | solution.py:254
  165.4 5.8 %collective-permute-start.20 = (bf16[32,4096]{1,0:T(8,128)(2,1)S(1)}, bf16[32,4096]{1,0:T(8,128)(2,1)S(1)}, u32[]{:S(2)}, u32[]{:S(2)}) collective-permute-start(bf16[32,4096]{1,0:T(8,128)(2,1)S(1)} %get-tuple-element.49), channel_id=1, source_target_pairs={{0,4},{2,6},{4,0},{6,2},{8,12},{10,14},{12,8},{14,10},{1,5},{3,7},... | collective-permute-start | bytes 786440 | tf_op jit(solution)/shard_map/ppermute | solution.py:326
  171.2 2.8 %copy-done.1 = bf16[384,64,128]{2,1,0:T(8,128)(2,1)S(1)} copy-done((bf16[384,64,128]{2,1,0:T(8,128)(2,1)S(1)}, bf16[384,64,128]{2,1,0:T(8,128)(2,1)}, u32[]{:S(2)}) %copy-start.1) | copy-done | bytes 6291480
  174.0 3.0 %shard_map.72 = (bf16[32,4096]{1,0:T(8,128)(2,1)S(1)}, bf16[32,4096]{1,0:T(8,128)(2,1)S(1)}, bf16[32,4096]{1,0:T(8,128)(2,1)S(1)}, bf16[32,4096]{1,0:T(8,128)(2,1)S(1)}) custom-call(s32[1289]{0:T(1024)S(1)} %concatenate.26.meta, bf16[32,4096]{1,0:T(8,128)(2,1)S(1)} %shard_map.70.refs_0_, bf16[32,4096]{1,0:T(8,128)(2,1)S(1)} %collective-permute-done.16.refs_1_, ...), custom_call_target="tpu_custom_call" | custom-call | flops 1 | bytes 1 | tf_op jit(solution)/shard_map/pallas_call | solution.py:254
  178.5 2.0 %collective-permute-start.23 = (bf16[32,4096]{1,0:T(8,128)(2,1)S(1)}, bf16[32,4096]{1,0:T(8,128)(2,1)S(1)}, u32[]{:S(2)}, u32[]{:S(2)}) collective-permute-start(bf16[32,4096]{1,0:T(8,128)(2,1)S(1)} %get-tuple-element.53), channel_id=1, source_target_pairs={{0,4},{2,6},{4,0},{6,2},{8,12},{10,14},{12,8},{14,10},{1,5},{3,7},... | collective-permute-start | bytes 786440 | tf_op jit(solution)/shard_map/ppermute | solution.py:326
  180.8 2.2 %collective-permute-done.21 = bf16[32,4096]{1,0:T(8,128)(2,1)S(1)} collective-permute-done((bf16[32,4096]{1,0:T(8,128)(2,1)S(1)}, bf16[32,4096]{1,0:T(8,128)(2,1)S(1)}, u32[]{:S(2)}, u32[]{:S(2)}) %collective-permute-start.21) | collective-permute-done | bytes 262176 | tf_op jit(solution)/shard_map/ppermute | solution.py:326
  183.1 4.7 %collective-permute-done.22 = bf16[32,4096]{1,0:T(8,128)(2,1)S(1)} collective-permute-done((bf16[32,4096]{1,0:T(8,128)(2,1)S(1)}, bf16[32,4096]{1,0:T(8,128)(2,1)S(1)}, u32[]{:S(2)}, u32[]{:S(2)}) %collective-permute-start.22) | collective-permute-done | bytes 262176 | tf_op jit(solution)/shard_map/ppermute | solution.py:326
  189.3 2.7 %collective-permute-done.24 = bf16[32,4096]{1,0:T(8,128)(2,1)S(1)} collective-permute-done((bf16[32,4096]{1,0:T(8,128)(2,1)S(1)}, bf16[32,4096]{1,0:T(8,128)(2,1)S(1)}, u32[]{:S(2)}, u32[]{:S(2)}) %collective-permute-start.24) | collective-permute-done | bytes 262176 | tf_op jit(solution)/shard_map/ppermute | solution.py:326
  (120 shorter events, 42.9 us)
Async XLA Ops:
  1.9 26.1 %collective-permute-start = (bf16[30,64,128]{2,1,0:T(8,128)(2,1)}, bf16[30,64,128]{2,1,0:T(8,128)(2,1)}, u32[]{:S(2)}, u32[]{:S(2)}) collective-permute-start(bf16[30,64,128]{2,1,0:T(8,128)(2,1)} %constant_dynamic-slice_fusion.4), channel_id=1, source_target_pairs={{0,8},{2,10},{4,12},{6,14},{8,0},{10,2},{12,4},{14,6},{1,9},{3,11}... | collective-permute-start | bytes 1474568 | tf_op jit(solution)/shard_map/ppermute | solution.py:364
  29.0 22.7 %all-to-all-start = ((bf16[32,4,4096]{2,0,1:T(8,128)(2,1)}), bf16[32,4,4096]{2,0,1:T(8,128)(2,1)S(1)}, u32[]{:S(2)}, u32[]{:S(2)}) async-start(bf16[32,4,4096]{2,0,1:T(8,128)(2,1)} %bitcast.20), calls=%async_computation | async-start | bytes 2097152 | tf_op jit(solution)/shard_map/all_to_all | solution.py:335
  36.3 8.9 %collective-permute-start.1 = (s32[3,384]{1,0:T(4,128)S(1)}, s32[3,384]{1,0:T(4,128)S(1)}, u32[]{:S(2)}, u32[]{:S(2)}) collective-permute-start(s32[3,384]{1,0:T(4,128)S(1)} %add_add_fusion), channel_id=1, source_target_pairs={{0,8},{2,10},{4,12},{6,14},{8,0},{10,2},{12,4},{14,6},{1,9},{3,11}... | collective-permute-start | bytes 13832 | tf_op jit(solution)/shard_map/ppermute | solution.py:368
  39.8 40.1 %collective-permute-start.2 = (bf16[34,64,128]{2,1,0:T(8,128)(2,1)}, bf16[34,64,128]{2,1,0:T(8,128)(2,1)}, u32[]{:S(2)}, u32[]{:S(2)}) collective-permute-start(bf16[34,64,128]{2,1,0:T(8,128)(2,1)} %constant_dynamic-slice_fusion.3), channel_id=1, source_target_pairs={{0,8},{2,10},{4,12},{6,14},{8,0},{10,2},{12,4},{14,6},{1,9},{3,11}... | collective-permute-start | bytes 1671176 | tf_op jit(solution)/shard_map/ppermute | solution.py:364
  39.9 60.0 %collective-permute-start.4 = (bf16[32,64,128]{2,1,0:T(8,128)(2,1)}, bf16[32,64,128]{2,1,0:T(8,128)(2,1)}, u32[]{:S(2)}, u32[]{:S(2)}) collective-permute-start(bf16[32,64,128]{2,1,0:T(8,128)(2,1)} %constant_dynamic-slice_fusion.2), channel_id=1, source_target_pairs={{0,8},{2,10},{4,12},{6,14},{8,0},{10,2},{12,4},{14,6},{1,9},{3,11}... | collective-permute-start | bytes 1572872 | tf_op jit(solution)/shard_map/ppermute | solution.py:364
  42.7 16.1 %collective-permute-start.3 = (bf16[30,64,128]{2,1,0:T(8,128)(2,1)}, bf16[30,64,128]{2,1,0:T(8,128)(2,1)}, u32[]{:S(2)}, u32[]{:S(2)}) collective-permute-start(bf16[30,64,128]{2,1,0:T(8,128)(2,1)} %collective-permute-done.refs_0_.refs_4_), channel_id=1, source_target_pairs={{0,16},{16,0},{1,17},{17,1},{2,18},{18,2},{3,19},{19,3},{4,20},{20... | collective-permute-start | bytes 1474568 | tf_op jit(solution)/shard_map/ppermute | solution.py:394
  54.4 45.5 %all-to-all-start.1 = ((bf16[32,4,4096]{2,0,1:T(8,128)(2,1)}), bf16[32,4,4096]{2,0,1:T(8,128)(2,1)S(1)}, u32[]{:S(2)}, u32[]{:S(2)}) async-start(bf16[32,4,4096]{2,0,1:T(8,128)(2,1)} %bitcast.26), calls=%async_computation.1 | async-start | bytes 2097152 | tf_op jit(solution)/shard_map/all_to_all | solution.py:335
  79.8 11.9 %collective-permute-start.5 = (bf16[34,64,128]{2,1,0:T(8,128)(2,1)}, bf16[34,64,128]{2,1,0:T(8,128)(2,1)}, u32[]{:S(2)}, u32[]{:S(2)}) collective-permute-start(bf16[34,64,128]{2,1,0:T(8,128)(2,1)} %collective-permute-done.2.refs_4_.refs_8_), channel_id=1, source_target_pairs={{0,16},{16,0},{1,17},{17,1},{2,18},{18,2},{3,19},{19,3},{4,20},{20... | collective-permute-start | bytes 1671176 | tf_op jit(solution)/shard_map/ppermute | solution.py:394
  83.5 30.9 %collective-permute-start.11 = (bf16[34,64,128]{2,1,0:T(8,128)(2,1)}, bf16[34,64,128]{2,1,0:T(8,128)(2,1)}, u32[]{:S(2)}, u32[]{:S(2)}) collective-permute-start(bf16[34,64,128]{2,1,0:T(8,128)(2,1)} %collective-permute-done.2.refs_4_.refs_8_), channel_id=1, source_target_pairs={{0,1},{1,0},{2,3},{3,2},{4,5},{5,4},{6,7},{7,6},{8,9},{9,8},{10,11... | collective-permute-start | bytes 1671176 | tf_op jit(solution)/shard_map/ppermute | solution.py:396
  91.7 22.7 %collective-permute-start.12 = (bf16[34,64,128]{2,1,0:T(8,128)(2,1)}, bf16[34,64,128]{2,1,0:T(8,128)(2,1)}, u32[]{:S(2)}, u32[]{:S(2)}) collective-permute-start(bf16[34,64,128]{2,1,0:T(8,128)(2,1)} %collective-permute-done.5.refs_5_.refs_9_), channel_id=1, source_target_pairs={{0,1},{1,0},{2,3},{3,2},{4,5},{5,4},{6,7},{7,6},{8,9},{9,8},{10,11... | collective-permute-start | bytes 1671176 | tf_op jit(solution)/shard_map/ppermute | solution.py:396
  99.9 14.5 %collective-permute-start.6 = (bf16[32,64,128]{2,1,0:T(8,128)(2,1)}, bf16[32,64,128]{2,1,0:T(8,128)(2,1)S(1)}, u32[]{:S(2)}, u32[]{:S(2)}) collective-permute-start(bf16[32,64,128]{2,1,0:T(8,128)(2,1)} %collective-permute-done.4.refs_0_.refs_12_), channel_id=1, source_target_pairs={{0,16},{16,0},{1,17},{17,1},{2,18},{18,2},{3,19},{19,3},{4,20},{20... | collective-permute-start | bytes 1572872 | tf_op jit(solution)/shard_map/ppermute | solution.py:394
  101.4 2.1 %collective-permute-start.9 = (bf16[30,64,128]{2,1,0:T(8,128)(2,1)}, bf16[30,64,128]{2,1,0:T(8,128)(2,1)S(1)}, u32[]{:S(2)}, u32[]{:S(2)}) collective-permute-start(bf16[30,64,128]{2,1,0:T(8,128)(2,1)} %collective-permute-done.refs_0_.refs_4_), channel_id=1, source_target_pairs={{0,1},{1,0},{2,3},{3,2},{4,5},{5,4},{6,7},{7,6},{8,9},{9,8},{10,11... | collective-permute-start | bytes 1474568 | tf_op jit(solution)/shard_map/ppermute | solution.py:396
  101.6 12.8 %collective-permute-start.10 = (bf16[30,64,128]{2,1,0:T(8,128)(2,1)}, bf16[30,64,128]{2,1,0:T(8,128)(2,1)S(1)}, u32[]{:S(2)}, u32[]{:S(2)}) collective-permute-start(bf16[30,64,128]{2,1,0:T(8,128)(2,1)} %collective-permute-done.3.refs_1_.refs_5_), channel_id=1, source_target_pairs={{0,1},{1,0},{2,3},{3,2},{4,5},{5,4},{6,7},{7,6},{8,9},{9,8},{10,11... | collective-permute-start | bytes 1474568 | tf_op jit(solution)/shard_map/ppermute | solution.py:396
  103.5 18.6 %copy-start.12 = (bf16[30,64,128]{2,1,0:T(8,128)(2,1)}, bf16[30,64,128]{2,1,0:T(8,128)(2,1)S(1)}, u32[]{:S(2)}) copy-start(bf16[30,64,128]{2,1,0:T(8,128)(2,1)S(1)} %collective-permute-done.9.refs_2_.refs_6_) | copy-start | bytes 1474564
  103.5 18.7 %collective-permute-start.7 = (bf16[32,64,128]{2,1,0:T(8,128)(2,1)}, bf16[32,64,128]{2,1,0:T(8,128)(2,1)S(1)}, u32[]{:S(2)}, u32[]{:S(2)}) collective-permute-start(bf16[32,64,128]{2,1,0:T(8,128)(2,1)} %collective-permute-done.4.refs_0_.refs_12_), channel_id=1, source_target_pairs={{0,1},{1,0},{2,3},{3,2},{4,5},{5,4},{6,7},{7,6},{8,9},{9,8},{10,11... | collective-permute-start | bytes 1572872 | tf_op jit(solution)/shard_map/ppermute | solution.py:396
  114.4 7.7 %copy-start.4 = (bf16[32,64,128]{2,1,0:T(8,128)(2,1)}, bf16[32,64,128]{2,1,0:T(8,128)(2,1)S(1)}, u32[]{:S(2)}) copy-start(bf16[32,64,128]{2,1,0:T(8,128)(2,1)S(1)} %collective-permute-done.6.refs_1_.refs_13_) | copy-start | bytes 1572868
  114.4 7.7 %collective-permute-start.8 = (bf16[32,64,128]{2,1,0:T(8,128)(2,1)S(1)}, bf16[32,64,128]{2,1,0:T(8,128)(2,1)S(1)}, u32[]{:S(2)}, u32[]{:S(2)}) collective-permute-start(bf16[32,64,128]{2,1,0:T(8,128)(2,1)S(1)} %collective-permute-done.6.refs_1_.refs_13_), channel_id=1, source_target_pairs={{0,1},{1,0},{2,3},{3,2},{4,5},{5,4},{6,7},{7,6},{8,9},{9,8},{10,11... | collective-permute-start | bytes 1572872 | tf_op jit(solution)/shard_map/ppermute | solution.py:396
  114.4 7.7 %copy-start.14 = (bf16[30,64,128]{2,1,0:T(8,128)(2,1)}, bf16[30,64,128]{2,1,0:T(8,128)(2,1)S(1)}, u32[]{:S(2)}) copy-start(bf16[30,64,128]{2,1,0:T(8,128)(2,1)S(1)} %collective-permute-done.10.refs_3_.refs_7_) | copy-start | bytes 1474564
  124.1 31.3 %copy-start.5 = (bf16[32,64,128]{2,1,0:T(8,128)(2,1)S(1)}, bf16[32,64,128]{2,1,0:T(8,128)(2,1)}, u32[]{:S(2)}) copy-start(bf16[32,64,128]{2,1,0:T(8,128)(2,1)} %copy-done.4) | copy-start | bytes 1572868
  124.1 31.3 %copy-start.7 = (bf16[32,64,128]{2,1,0:T(8,128)(2,1)S(1)}, bf16[32,64,128]{2,1,0:T(8,128)(2,1)}, u32[]{:S(2)}) copy-start(bf16[32,64,128]{2,1,0:T(8,128)(2,1)} %copy-done.6) | copy-start | bytes 1572868
  124.1 8.6 %collective-permute-start.13 = (bf16[32,4096]{1,0:T(8,128)(2,1)S(1)}, bf16[32,4096]{1,0:T(8,128)(2,1)S(1)}, u32[]{:S(2)}, u32[]{:S(2)}) collective-permute-start(bf16[32,4096]{1,0:T(8,128)(2,1)S(1)} %get-tuple-element.44), channel_id=1, source_target_pairs={{0,2},{2,0},{4,6},{6,4},{8,10},{10,8},{12,14},{14,12},{1,3},{3,1},... | collective-permute-start | bytes 786440 | tf_op jit(solution)/shard_map/ppermute | solution.py:326
  124.8 10.2 %collective-permute-start.14 = (bf16[32,4096]{1,0:T(8,128)(2,1)S(1)}, bf16[32,4096]{1,0:T(8,128)(2,1)S(1)}, u32[]{:S(2)}, u32[]{:S(2)}) collective-permute-start(bf16[32,4096]{1,0:T(8,128)(2,1)S(1)} %get-tuple-element.45), channel_id=1, source_target_pairs={{0,4},{2,6},{4,0},{6,2},{8,12},{10,14},{12,8},{14,10},{1,5},{3,7},... | collective-permute-start | bytes 786440 | tf_op jit(solution)/shard_map/ppermute | solution.py:326
  127.9 11.9 %collective-permute-start.15 = (bf16[32,4096]{1,0:T(8,128)(2,1)S(1)}, bf16[32,4096]{1,0:T(8,128)(2,1)S(1)}, u32[]{:S(2)}, u32[]{:S(2)}) collective-permute-start(bf16[32,4096]{1,0:T(8,128)(2,1)S(1)} %get-tuple-element.46), channel_id=1, source_target_pairs={{0,6},{2,4},{4,2},{6,0},{8,14},{10,12},{12,10},{14,8},{1,7},{3,5},... | collective-permute-start | bytes 786440 | tf_op jit(solution)/shard_map/ppermute | solution.py:326
  140.8 8.4 %collective-permute-start.16 = (bf16[32,4096]{1,0:T(8,128)(2,1)S(1)}, bf16[32,4096]{1,0:T(8,128)(2,1)S(1)}, u32[]{:S(2)}, u32[]{:S(2)}) collective-permute-start(bf16[32,4096]{1,0:T(8,128)(2,1)S(1)} %shard_map.70.refs_0_), channel_id=1, source_target_pairs={{0,2},{2,0},{4,6},{6,4},{8,10},{10,8},{12,14},{14,12},{1,3},{3,1},... | collective-permute-start | bytes 786440 | tf_op jit(solution)/shard_map/ppermute | solution.py:326
  142.5 9.2 %collective-permute-start.17 = (bf16[32,4096]{1,0:T(8,128)(2,1)S(1)}, bf16[32,4096]{1,0:T(8,128)(2,1)S(1)}, u32[]{:S(2)}, u32[]{:S(2)}) collective-permute-start(bf16[32,4096]{1,0:T(8,128)(2,1)S(1)} %shard_map.70.refs_0_), channel_id=1, source_target_pairs={{0,4},{2,6},{4,0},{6,2},{8,12},{10,14},{12,8},{14,10},{1,5},{3,7},... | collective-permute-start | bytes 786440 | tf_op jit(solution)/shard_map/ppermute | solution.py:326
  144.2 11.2 %collective-permute-start.18 = (bf16[32,4096]{1,0:T(8,128)(2,1)S(1)}, bf16[32,4096]{1,0:T(8,128)(2,1)S(1)}, u32[]{:S(2)}, u32[]{:S(2)}) collective-permute-start(bf16[32,4096]{1,0:T(8,128)(2,1)S(1)} %shard_map.70.refs_0_), channel_id=1, source_target_pairs={{0,6},{2,4},{4,2},{6,0},{8,14},{10,12},{12,10},{14,8},{1,7},{3,5},... | collective-permute-start | bytes 786440 | tf_op jit(solution)/shard_map/ppermute | solution.py:326
  164.6 16.1 %collective-permute-start.19 = (bf16[32,4096]{1,0:T(8,128)(2,1)S(1)}, bf16[32,4096]{1,0:T(8,128)(2,1)S(1)}, u32[]{:S(2)}, u32[]{:S(2)}) collective-permute-start(bf16[32,4096]{1,0:T(8,128)(2,1)S(1)} %get-tuple-element.48), channel_id=1, source_target_pairs={{0,2},{2,0},{4,6},{6,4},{8,10},{10,8},{12,14},{14,12},{1,3},{3,1},... | collective-permute-start | bytes 786440 | tf_op jit(solution)/shard_map/ppermute | solution.py:326
  165.4 15.4 %collective-permute-start.20 = (bf16[32,4096]{1,0:T(8,128)(2,1)S(1)}, bf16[32,4096]{1,0:T(8,128)(2,1)S(1)}, u32[]{:S(2)}, u32[]{:S(2)}) collective-permute-start(bf16[32,4096]{1,0:T(8,128)(2,1)S(1)} %get-tuple-element.49), channel_id=1, source_target_pairs={{0,4},{2,6},{4,0},{6,2},{8,12},{10,14},{12,8},{14,10},{1,5},{3,7},... | collective-permute-start | bytes 786440 | tf_op jit(solution)/shard_map/ppermute | solution.py:326
  171.2 11.9 %collective-permute-start.21 = (bf16[32,4096]{1,0:T(8,128)(2,1)S(1)}, bf16[32,4096]{1,0:T(8,128)(2,1)S(1)}, u32[]{:S(2)}, u32[]{:S(2)}) collective-permute-start(bf16[32,4096]{1,0:T(8,128)(2,1)S(1)} %get-tuple-element.50), channel_id=1, source_target_pairs={{0,6},{2,4},{4,2},{6,0},{8,14},{10,12},{12,10},{14,8},{1,7},{3,5},... | collective-permute-start | bytes 786440 | tf_op jit(solution)/shard_map/ppermute | solution.py:326
  177.0 10.8 %collective-permute-start.22 = (bf16[32,4096]{1,0:T(8,128)(2,1)S(1)}, bf16[32,4096]{1,0:T(8,128)(2,1)S(1)}, u32[]{:S(2)}, u32[]{:S(2)}) collective-permute-start(bf16[32,4096]{1,0:T(8,128)(2,1)S(1)} %get-tuple-element.52), channel_id=1, source_target_pairs={{0,2},{2,0},{4,6},{6,4},{8,10},{10,8},{12,14},{14,12},{1,3},{3,1},... | collective-permute-start | bytes 786440 | tf_op jit(solution)/shard_map/ppermute | solution.py:326
  178.5 10.7 %collective-permute-start.23 = (bf16[32,4096]{1,0:T(8,128)(2,1)S(1)}, bf16[32,4096]{1,0:T(8,128)(2,1)S(1)}, u32[]{:S(2)}, u32[]{:S(2)}) collective-permute-start(bf16[32,4096]{1,0:T(8,128)(2,1)S(1)} %get-tuple-element.53), channel_id=1, source_target_pairs={{0,4},{2,6},{4,0},{6,2},{8,12},{10,14},{12,8},{14,10},{1,5},{3,7},... | collective-permute-start | bytes 786440 | tf_op jit(solution)/shard_map/ppermute | solution.py:326
  180.7 11.3 %collective-permute-start.24 = (bf16[32,4096]{1,0:T(8,128)(2,1)S(1)}, bf16[32,4096]{1,0:T(8,128)(2,1)S(1)}, u32[]{:S(2)}, u32[]{:S(2)}) collective-permute-start(bf16[32,4096]{1,0:T(8,128)(2,1)S(1)} %get-tuple-element.54), channel_id=1, source_target_pairs={{0,6},{2,4},{4,2},{6,0},{8,14},{10,12},{12,10},{14,8},{1,7},{3,5},... | collective-permute-start | bytes 786440 | tf_op jit(solution)/shard_map/ppermute | solution.py:326
  (13 other events, 27.6 us)
